TPU v7x, 32 devices: a whole 2x2x4 slice. The times are simulated.
32 devices in a mesh: row: 8 (over z, x), col: 4 (over y, core).
Axes of the slice: x: 2, y: 2, z: 4, core: 2. Of those that a mesh axis runs over, the one named last changes fastest.
Arguments:
- panel_block: float32 [16384, 128], P('row'), may hold values from -8 to 8, as said below
- trailing: float32 [16384, 16384], P('row', 'col'), may hold values from -80 to 80
Outputs:
- reduced: float32 [16384, 16384], P('row', 'col')
- band_block: float32 [128, 128], replicated
- first_factor: float32 [128, 128], replicated
Inputs may be any that keep to these rules, and one draw needn't show every extreme that they name: `panel_block`: entries of order the inverse square root of 16384; rows may differ in scale; the columns may be nearly dependent, with a condition number of the panel up to a few thousand; the first 128 rows of the orthonormal basis have spectral norm at most 0.8, so that I + top^T needs no pivoting.
All inputs are finite; a program needn't handle non-finite values.
Results may differ from a plain program's by a relative error of at most 0.0017.
Values sent between devices are 32-bit elements; how exact they have to be, the bound alone decides.
No kernel may reach another device: no remote copies, remote signals or barrier semaphores. Data moves between devices by JAX's collectives and lax.ppermute only.
A program may use at most 128 MiB of HBM per device.

v0:
```python
import jax
import jax.numpy as jnp
from jax import lax
from jax.sharding import PartitionSpec as P

HIGH = lax.Precision.HIGHEST


def broadcast(shard, axis, root):
    mine = lax.axis_index(axis) == root
    return lax.psum(jnp.where(mine, shard, jnp.zeros_like(shard)), axis)


def gram_of(values):
    return lax.dot_general(
        values, values, (((0,), (0,)), ((), ())), precision=HIGH, preferred_element_type=jnp.float32
    )


def times_of(left, right):
    return jnp.dot(left, right, precision=HIGH, preferred_element_type=jnp.float32)


def outer_of(left, right):
    return lax.dot_general(
        left, right, (((1,), (1,)), ((), ())), precision=HIGH, preferred_element_type=jnp.float32
    )


def gram_both(left, right):
    return lax.dot_general(
        left, right, (((0,), (0,)), ((), ())), precision=HIGH, preferred_element_type=jnp.float32
    )


def eliminate_small(square):
    size_n = square.shape[0]
    augmented = jnp.concatenate([square, jnp.eye(size_n, dtype=square.dtype)], axis=1)
    positions = jnp.arange(size_n)

    def eliminate(pivot, current):
        pivot_row = lax.dynamic_index_in_dim(current, pivot, 0, keepdims=False)
        pivot_row = pivot_row / pivot_row[pivot]
        column = lax.dynamic_index_in_dim(current, pivot, 1, keepdims=False)
        column = column - (positions == pivot).astype(current.dtype)
        return current - column[:, None] * pivot_row[None, :]

    augmented = lax.fori_loop(0, size_n, eliminate, augmented)
    return augmented[:, size_n:]


def invert_square(square):
    size_n = square.shape[0]
    if size_n <= 16:
        return eliminate_small(square)
    half = size_n // 2
    upper_left = square[:half, :half]
    upper_right = square[:half, half:]
    lower_left = square[half:, :half]
    lower_right = square[half:, half:]
    left_inverse = invert_square(upper_left)
    left_times_right = times_of(left_inverse, upper_right)
    lower_times_left = times_of(lower_left, left_inverse)
    schur = lower_right - times_of(lower_left, left_times_right)
    schur_inverse = invert_square(schur)
    top_right = -times_of(left_times_right, schur_inverse)
    bottom_left = -times_of(schur_inverse, lower_times_left)
    top_left = left_inverse - times_of(top_right, lower_times_left)
    upper = jnp.concatenate([top_left, top_right], axis=1)
    lower = jnp.concatenate([bottom_left, schur_inverse], axis=1)
    return jnp.concatenate([upper, lower], axis=0)


def right_solve(factor, values):
    return lax.linalg.triangular_solve(
        factor, values, left_side=False, lower=True, transpose_a=True
    )


def body(panel_block, trailing):
    shard_rows = panel_block.shape[0]
    panel_width = panel_block.shape[1]
    col_count = trailing.shape[1]
    row_index = lax.axis_index("row")
    col_index = lax.axis_index("col")
    ratio = lax.axis_size("row") // lax.axis_size("col")
    first_gram = lax.psum(gram_of(panel_block), "row")
    first_factor = jnp.linalg.cholesky(first_gram)
    first_basis = right_solve(first_factor, panel_block)
    second_gram = lax.psum(gram_of(first_basis), "row")
    second_factor = jnp.linalg.cholesky(second_gram)
    basis = right_solve(second_factor, first_basis)
    top_basis = broadcast(basis[:panel_width], "row", 0)
    band_block = -times_of(second_factor.T, first_factor.T)
    kernel = invert_square(jnp.eye(panel_width, dtype=jnp.float32) + top_basis.T)
    global_rows = row_index * shard_rows + jnp.arange(shard_rows)
    ident = (global_rows[:, None] == jnp.arange(panel_width)[None, :]).astype(jnp.float32)
    vectors = basis + ident
    partial_product = lax.dot_general(
        trailing,
        vectors,
        (((0,), (0,)), ((), ())),
        precision=HIGH,
        preferred_element_type=jnp.float32,
    )
    placed = lax.dynamic_update_slice_in_dim(
        jnp.zeros((col_count, panel_width), jnp.float32), vectors, row_index % ratio * shard_rows, 0
    )
    placed = jnp.where(row_index // ratio == col_index, placed, jnp.zeros_like(placed))
    col_product, col_vectors = lax.psum((partial_product, placed), "row")
    applied = times_of(col_product, kernel)
    inner_sum = lax.psum(gram_both(col_vectors, applied), "col")
    inner = times_of(kernel.T, inner_sum)
    col_update = applied - 0.5 * times_of(col_vectors, inner)
    own_piece = lax.dynamic_slice_in_dim(col_update, row_index % ratio * shard_rows, shard_rows, 0)
    row_update = broadcast(own_piece, "col", row_index // ratio)
    reduced = trailing - outer_of(vectors, col_update) - outer_of(row_update, col_vectors)
    return (reduced, band_block, first_factor)


def solution(mesh):
    in_specs = (P("row", None), P("row", "col"))
    out_specs = (P("row", "col"), P(), P())
    return jax.shard_map(body, mesh=mesh, in_specs=in_specs, out_specs=out_specs, check_vma=False)
```

profile of v0, /device:TPU:12, one launch (start us, length us, event | category | flops | bytes accessed | tf_op | source)
XLA Modules:
  0.0 721.8 jit_solution(13772865272041246916)
XLA Ops:
  10.9 70.9 %all-reduce.7.cloned.1.call-done = f32[128,128]{0,1:T(8,128)} async-done(((f32[128,128]{0,1:T(8,128)}), f32[128,128]{0,1:T(8,128)}) %all-reduce.7.cloned.1.call-update) | async-done | bytes 65552 | tf_op jit(solution)/shard_map/psum | solution.py:87
  83.6 11.7 %cholesky.44 = f32[128,128]{1,0:T(8,128)S(1)} custom-call(f32[128,128]{1,0:T(8,128)S(1)} %fusion.56), custom_call_target="Cholesky" | custom-call | tf_op jit(solution)/shard_map/jit(cholesky)/cholesky | solution.py:88
  96.7 9.8 %custom-call.6 = f32[1,128,128]{1,2,0:T(8,128)S(1)} custom-call(f32[1,128,128]{2,1,0:T(8,128)S(1)} %get-tuple-element.928), custom_call_target="InvertDiagBlocksLowerTriangular" | custom-call | tf_op jit(solution)/shard_map/triangular_solve/custom-call.0 | solution.py:75
  109.8 68.1 %all-reduce.9.cloned.1.call-done = f32[128,128]{0,1:T(8,128)} async-done(((f32[128,128]{0,1:T(8,128)}), f32[128,128]{0,1:T(8,128)}) %all-reduce.9.cloned.1.call-update) | async-done | bytes 65552 | tf_op jit(solution)/shard_map/psum | solution.py:90
  179.6 11.7 %cholesky.55 = f32[128,128]{1,0:T(8,128)S(1)} custom-call(f32[128,128]{1,0:T(8,128)S(1)} %fusion.54), custom_call_target="Cholesky" | custom-call | tf_op jit(solution)/shard_map/jit(cholesky)/cholesky | solution.py:91
  192.6 9.8 %custom-call.7 = f32[1,128,128]{1,2,0:T(8,128)S(1)} custom-call(f32[1,128,128]{2,1,0:T(8,128)S(1)} %select_bitcast_fusion), custom_call_target="InvertDiagBlocksLowerTriangular" | custom-call | tf_op jit(solution)/shard_map/triangular_solve/custom-call.0 | solution.py:75
  205.1 22.8 %convolution_bitcast_fusion = f32[4096,128]{0,1:T(8,128)} fusion(f32[2048,4096]{1,0:T(8,128)} %param.22, f32[2048,128]{0,1:T(8,128)S(1)} %get-tuple-element.931, s32[2048]{0:T(1024)S(1)} %iota_add_fusion), kind=kOutput, calls=%fused_computation.67 | convolution fusion | flops 12885688320 | bytes 36708352 | tf_op jit(solution)/shard_map/dot_general | solution.py:99
  228.7 156.5 %all-reduce.15.cloned.1.call-done = (f32[4096,128]{0,1:T(8,128)}, f32[128,128]{1,0:T(8,128)}, f32[4096,128]{0,1:T(8,128)}) async-done(((f32[4096,128]{0,1:T(8,128)}, f32[128,128]{1,0:T(8,128)}, f32[4096,128]{0,1:T(8,128)}), (f32[4096,128]{0,1:T(8,128)}, f32[128,128]{1,0:T(8,128)}, f32[4096,128]{0,1:T(8,128)})) %all-reduce.15.cloned.1.call-update) | async-done | bytes 4259856 | tf_op jit(solution)/shard_map/psum | solution.py:110
  386.3 24.0 %while.136 = (s32[]{:T(128)}, f32[16,32]{0,1:T(8,128)S(1)}, s32[]{:T(128)}, s32[]{:T(128)}, s32[]{:T(128)}, /*index=5*/s32[]{:T(128)}) while((s32[]{:T(128)}, f32[16,32]{0,1:T(8,128)S(1)}, s32[]{:T(128)}, s32[]{:T(128)}, s32[]{:T(128)}, /*index=5*/s32[]{:T(128)}) %tuple.325), condition=%wide.region_7.10_spmd.clone, body=%wide.region_6.9_spmd.clone.sunk | while | flops 1108 | bytes 5817 | solution.py:48
  411.1 24.0 %while.137 = (s32[]{:T(128)}, f32[16,32]{0,1:T(8,128)S(1)}, s32[]{:T(128)}, s32[]{:T(128)}, s32[]{:T(128)}, /*index=5*/s32[]{:T(128)}) while((s32[]{:T(128)}, f32[16,32]{0,1:T(8,128)S(1)}, s32[]{:T(128)}, s32[]{:T(128)}, s32[]{:T(128)}, /*index=5*/s32[]{:T(128)}) %tuple.328), condition=%wide.region_9.12_spmd.clone, body=%wide.region_8.11_spmd.clone.sunk | while | flops 1108 | bytes 5817 | solution.py:48
  436.3 24.0 %while.138 = (s32[]{:T(128)}, f32[16,32]{0,1:T(8,128)S(1)}, s32[]{:T(128)}, s32[]{:T(128)}, s32[]{:T(128)}, /*index=5*/s32[]{:T(128)}) while((s32[]{:T(128)}, f32[16,32]{0,1:T(8,128)S(1)}, s32[]{:T(128)}, s32[]{:T(128)}, s32[]{:T(128)}, /*index=5*/s32[]{:T(128)}) %tuple.331), condition=%wide.region_11.14_spmd.clone, body=%wide.region_10.13_spmd.clone.sunk | while | flops 1108 | bytes 5817 | solution.py:48
  461.1 24.0 %while.139 = (s32[]{:T(128)}, f32[16,32]{0,1:T(8,128)S(1)}, s32[]{:T(128)}, s32[]{:T(128)}, s32[]{:T(128)}, /*index=5*/s32[]{:T(128)}) while((s32[]{:T(128)}, f32[16,32]{0,1:T(8,128)S(1)}, s32[]{:T(128)}, s32[]{:T(128)}, s32[]{:T(128)}, /*index=5*/s32[]{:T(128)}) %tuple.334), condition=%wide.region_13.16_spmd.clone, body=%wide.region_12.15_spmd.clone.sunk | while | flops 1108 | bytes 5817 | solution.py:48
  487.4 24.0 %while.140 = (s32[]{:T(128)}, f32[16,32]{0,1:T(8,128)S(1)}, s32[]{:T(128)}, s32[]{:T(128)}, s32[]{:T(128)}, /*index=5*/s32[]{:T(128)}) while((s32[]{:T(128)}, f32[16,32]{0,1:T(8,128)S(1)}, s32[]{:T(128)}, s32[]{:T(128)}, s32[]{:T(128)}, /*index=5*/s32[]{:T(128)}) %tuple.337), condition=%wide.region_15.18_spmd.clone, body=%wide.region_14.17_spmd.clone.sunk | while | flops 1108 | bytes 5817 | solution.py:48
  512.1 24.0 %while.141 = (s32[]{:T(128)}, f32[16,32]{0,1:T(8,128)S(1)}, s32[]{:T(128)}, s32[]{:T(128)}, s32[]{:T(128)}, /*index=5*/s32[]{:T(128)}) while((s32[]{:T(128)}, f32[16,32]{0,1:T(8,128)S(1)}, s32[]{:T(128)}, s32[]{:T(128)}, s32[]{:T(128)}, /*index=5*/s32[]{:T(128)}) %tuple.340), condition=%wide.region_17.20_spmd.clone, body=%wide.region_16.19_spmd.clone.sunk | while | flops 1108 | bytes 5817 | solution.py:48
  537.4 24.0 %while.142 = (s32[]{:T(128)}, f32[16,32]{0,1:T(8,128)S(1)}, s32[]{:T(128)}, s32[]{:T(128)}, s32[]{:T(128)}, /*index=5*/s32[]{:T(128)}) while((s32[]{:T(128)}, f32[16,32]{0,1:T(8,128)S(1)}, s32[]{:T(128)}, s32[]{:T(128)}, s32[]{:T(128)}, /*index=5*/s32[]{:T(128)}) %tuple.343), condition=%wide.region_19.22_spmd.clone, body=%wide.region_18.21_spmd.clone.sunk | while | flops 1108 | bytes 5817 | solution.py:48
  562.2 24.0 %while.143 = (s32[]{:T(128)}, f32[16,32]{0,1:T(8,128)S(1)}, s32[]{:T(128)}, s32[]{:T(128)}, s32[]{:T(128)}, /*index=5*/s32[]{:T(128)}) while((s32[]{:T(128)}, f32[16,32]{0,1:T(8,128)S(1)}, s32[]{:T(128)}, s32[]{:T(128)}, s32[]{:T(128)}, /*index=5*/s32[]{:T(128)}) %tuple.346), condition=%wide.region_21.24_spmd.clone, body=%wide.region_20.23_spmd.clone.sunk | while | flops 1108 | bytes 5817 | solution.py:48
  588.6 5.3 fusion.128
  595.2 2.8 fusion.132
  599.8 2.9 copy.48
  602.7 26.4 %all-reduce.11.cloned.1.call-done = f32[128,128]{1,0:T(8,128)} async-done(((f32[128,128]{1,0:T(8,128)}), f32[128,128]{1,0:T(8,128)}) %all-reduce.11.cloned.1.call-update) | async-done | bytes 65552 | tf_op jit(solution)/shard_map/psum | solution.py:112
  630.3 3.7 fusion.48
  636.4 31.4 %fusion.49 = f32[2048,4096]{1,0:T(8,128)} fusion(f32[4096,128]{0,1:T(8,128)} %copy-done.4, f32[2048,128]{0,1:T(8,128)S(1)} %get-tuple-element.931, s32[2048]{0:T(1024)S(1)} %iota_add_fusion), kind=kOutput, calls=%fused_computation.103 | convolution fusion | flops 12885688320 | bytes 36708352 | tf_op jit(solution)/shard_map/dot_general | solution.py:25
  667.8 5.3 all-reduce.13.cloned.1.call-done
  673.1 41.7 %subtract_subtract_fusion = f32[2048,4096]{1,0:T(8,128)} fusion(f32[2048,4096]{1,0:T(8,128)} %param.22, f32[2048,4096]{1,0:T(8,128)} %fusion.49, f32[2048,128]{0,1:T(8,128)} %all-reduce.13.cloned.1.call-done, f32[4096,128]{0,1:T(8,128)S(1)} %copy-done.2), kind=kOutput, calls=%fused_computation.64 | convolution fusion | flops 12901679104 | bytes 103809024 | tf_op jit(solution)/shard_map/dot_general | solution.py:25
  (633 shorter events, 225.4 us)
Async XLA Ops:
  7.2 1.2 copy-start
  7.2 74.6 %all-reduce.7.cloned.1.call-start = ((), (), s32[]{:S(2)}) async-start(), calls=%async_computation | async-start | bytes 131072 | tf_op jit(solution)/shard_map/psum | solution.py:87
  10.9 167.0 %all-reduce.9.cloned.1.call-start = ((), (), s32[]{:S(2)}) async-start(), calls=%async_computation.1 | async-start | bytes 131072 | tf_op jit(solution)/shard_map/psum | solution.py:90
  96.7 501.6 %copy-start.6 = (f32[128,128]{1,0:T(8,128)}, f32[128,128]{1,0:T(8,128)S(1)}, u32[]{:S(2)}) copy-start(f32[128,128]{1,0:T(8,128)S(1)} %get-tuple-element.929) | copy-start | bytes 196612
  109.2 276.0 %all-reduce.15.cloned.1.call-start = ((), (), s32[]{:S(2)}) async-start(), calls=%async_computation.4 | async-start | bytes 8519680 | tf_op jit(solution)/shard_map/psum | solution.py:110
  203.7 1.3 copy-start.5
  228.5 400.6 %all-reduce.11.cloned.1.call-start = ((), (), s32[]{:S(2)}) async-start(), calls=%async_computation.2 | async-start | bytes 131072 | tf_op jit(solution)/shard_map/psum | solution.py:112
  588.6 6.6 copy-start.2
  593.9 1.3 copy-start.3
  598.0 75.1 %all-reduce.13.cloned.1.call-start = ((), (), s32[]{:S(2)}) async-start(), calls=%async_computation.3 | async-start | bytes 2097152 | tf_op jit(solution)/shard_map/psum | solution.py:11
  634.0 1.4 copy-start.4
  673.1 41.7 %copy-start.1 = (f32[2048,128]{1,0:T(8,128)S(1)}, f32[2048,128]{1,0:T(8,128)}, u32[]{:S(2)}) copy-start(f32[2048,128]{1,0:T(8,128)} %param.21) | copy-start | bytes 3145732
Sparse Core Ops, SparseCore 0:
  12.0 69.7 all-reduce.6
  109.3 68.4 all-reduce.8
  228.6 156.5 all-reduce.14
  598.1 30.8 all-reduce.10
  636.6 36.5 all-reduce.12
where the time goes:
time: 733 us; the launch traced here: 722 us
  waiting for transfers between devices  327 us (45%)
  other arithmetic  167 us (23%)
  matrix products  124 us (17%)
  local copies, waits for them, and re-layouts  86.5 us (12%)
  between operations  14.6 us (2%)
    psum x1, waiting for transfers between devices, body(): col_product, col_vectors = lax.psum((partial_product, placed), 'row')  157 us
    div x128, other arithmetic, eliminate(): pivot_row = pivot_row / pivot_row[pivot]  105 us
    dynamic_slice x128, local copies, waits for them, and re-layouts, eliminate(): pivot_row = pivot_row / pivot_row[pivot]  74.9 us
    dot_general x2, matrix products, outer_of(): lax.dot_general(left, right, (((1,), (1,)), ((), ())), precision=HIGH, pr...  73.1 us
    psum x1, waiting for transfers between devices, body(): first_gram = lax.psum(gram_of(panel_block), 'row')  70.9 us
    psum x1, waiting for transfers between devices, body(): second_gram = lax.psum(gram_of(first_basis), 'row')  68.1 us
    psum x1, waiting for transfers between devices, body(): inner_sum = lax.psum(gram_both(col_vectors, applied), 'col')  26.4 us
    dot_general x1, matrix products, body(): lax.dot_general(trailing, vectors, (((0,), (0,)), ((), ())), precision=HI...  22.8 us
  transfers between devices with their start and end apart: 5, of which 5 were waited for; matrix products, arithmetic and copies ran while one was open for 5% of the time, Pallas kernels for 0%

commit v1 on v0

v1 whole, which is shorter than its diff:
```python
import functools

import jax
import jax.numpy as jnp
from jax import lax
from jax.experimental import pallas as pl
from jax.experimental.pallas import tpu as pltpu
from jax.sharding import PartitionSpec as P

HIGH = lax.Precision.HIGHEST
F32 = jnp.float32
BF16 = jnp.bfloat16
SUB = 8


def dot_nn(a, b):
    return lax.dot_general(a, b, (((1,), (0,)), ((), ())), precision=HIGH, preferred_element_type=F32)


def dot_nt(a, b):
    return lax.dot_general(a, b, (((1,), (1,)), ((), ())), precision=HIGH, preferred_element_type=F32)


def dot_tn(a, b):
    return lax.dot_general(a, b, (((0,), (0,)), ((), ())), precision=HIGH, preferred_element_type=F32)


def dot_fast(a, b):
    return lax.dot_general(a, b, (((1,), (0,)), ((), ())), preferred_element_type=F32)


def lane_copy(tile, lane):
    return jnp.broadcast_to(tile[:, lane : lane + 1], tile.shape)


def row_copy(tile, row):
    return jnp.broadcast_to(tile[row : row + 1, :], tile.shape)


def cholesky_tiles(tiles):
    size = tiles[0].shape[1]
    count = len(tiles)
    tiles = list(tiles)
    lanes = lax.broadcasted_iota(jnp.int32, (SUB, size), 1)
    subs = lax.broadcasted_iota(jnp.int32, (SUB, size), 0)
    upper, inverse = [], []
    for block in range(count):
        base = block * SUB
        here = (lanes >= base) & (lanes < base + SUB)
        columns = [[lane_copy(tiles[i], base + k) for k in range(SUB)] for i in range(block, count)]
        right = jnp.where(lanes >= base, tiles[block], 0.0)
        left = jnp.where(lanes < base, tiles[block], 0.0)
        left = jnp.where(lanes - base == subs, 1.0, left)
        out_upper, out_inverse = jnp.zeros_like(right), jnp.zeros_like(left)
        below = [jnp.where(here, 0.0, tiles[i]) for i in range(block + 1, count)]
        for k in range(SUB):
            diag = columns[0]
            pivot = row_copy(diag[k], k)
            root = lax.rsqrt(pivot)
            recip = 1.0 / pivot
            right_row, left_row = row_copy(right, k), row_copy(left, k)
            out_upper = jnp.where(subs == k, right_row * root, out_upper)
            out_inverse = jnp.where(subs == k, left_row * root, out_inverse)
            packed = jnp.where(lanes < base + SUB, left_row, right_row) * recip
            rows = {l: row_copy(diag[l], k) * recip for l in range(k + 1, SUB)}
            factor = jnp.where(subs > k, diag[k], 0.0)
            right = right - factor * (right_row * recip)
            left = left - factor * (left_row * recip)
            for i in range(count - block):
                for l in range(k + 1, SUB):
                    if i == 0:
                        columns[0][l] = columns[0][l] - factor * rows[l]
                    else:
                        columns[i][l] = columns[i][l] - columns[i][k] * rows[l]
                if i:
                    below[i - 1] = below[i - 1] - columns[i][k] * packed
        for i in range(block + 1, count):
            tiles[i] = below[i - block - 1]
        upper.append(jnp.where(lanes >= base + subs, out_upper, 0.0))
        inverse.append(out_inverse)
    return upper, inverse


def invert_tiles(tiles):
    size = tiles[0].shape[1]
    count = len(tiles)
    tiles = list(tiles)
    lanes = lax.broadcasted_iota(jnp.int32, (SUB, size), 1)
    subs = lax.broadcasted_iota(jnp.int32, (SUB, size), 0)
    for block in range(count):
        base = block * SUB
        here = (lanes >= base) & (lanes < base + SUB)
        columns = [[lane_copy(tiles[i], base + k) for k in range(SUB)] for i in range(count)]
        diag = list(columns[block])
        row = jnp.where(here, jnp.where(lanes - base == subs, 1.0, 0.0), tiles[block])
        for k in range(SUB):
            recip = 1.0 / row_copy(diag[k], k)
            own = subs == k
            pivot_row = row_copy(row, k) * recip
            rows = {l: row_copy(diag[l], k) * recip for l in range(k + 1, SUB)}
            row = jnp.where(own, pivot_row, row - diag[k] * pivot_row)
            for l in range(k + 1, SUB):
                diag[l] = jnp.where(own, rows[l], diag[l] - diag[k] * rows[l])
        spread = [row_copy(row, k) for k in range(SUB)]
        for i in range(count):
            if i == block:
                continue
            value = jnp.where(here, 0.0, tiles[i])
            for k in range(SUB):
                value = value - columns[i][k] * spread[k]
            tiles[i] = value
        tiles[block] = row
    return tiles


def tiles_of(ref):
    return [ref[i * SUB : (i + 1) * SUB, :] for i in range(ref.shape[0] // SUB)]


def first_kernel(gram_ref, panel_ref, factor_ref, inverse_ref, basis_ref, second_ref):
    upper, inverse = cholesky_tiles(tiles_of(gram_ref))
    factor_ref[...] = jnp.concatenate(upper, axis=0).T
    inverse_ref[...] = jnp.concatenate(inverse, axis=0)
    basis_ref[...] = dot_nt(panel_ref[...], inverse_ref[...])
    basis = basis_ref[...]
    second_ref[...] = dot_tn(basis, basis)


def first_pass(gram, panel):
    square = jax.ShapeDtypeStruct(gram.shape, F32)
    return pl.pallas_call(
        first_kernel,
        out_shape=(square, square, jax.ShapeDtypeStruct(panel.shape, F32), square),
        compiler_params=pltpu.CompilerParams(vmem_limit_bytes=32 * 1024 * 1024),
        name="first_pass",
    )(gram, panel)


def second_kernel(gram_ref, first_ref, top_ref, inverse_ref, band_ref, kernel_ref):
    upper, inverse = cholesky_tiles(tiles_of(gram_ref))
    inverse_ref[...] = jnp.concatenate(inverse, axis=0)
    band_ref[...] = -dot_nt(jnp.concatenate(upper, axis=0), first_ref[...])
    size = gram_ref.shape[0]
    rows = lax.broadcasted_iota(jnp.int32, (size, size), 0)
    lanes = lax.broadcasted_iota(jnp.int32, (size, size), 1)
    eye = jnp.where(rows == lanes, 1.0, 0.0)
    kernel_ref[...] = eye + dot_nt(inverse_ref[...], top_ref[...])
    kernel_ref[...] = jnp.concatenate(invert_tiles(tiles_of(kernel_ref)), axis=0)


def second_pass(gram, first_factor, top):
    square = jax.ShapeDtypeStruct(gram.shape, F32)
    return pl.pallas_call(
        second_kernel,
        out_shape=(square, square, square),
        compiler_params=pltpu.CompilerParams(vmem_limit_bytes=32 * 1024 * 1024),
        name="second_pass",
    )(gram, first_factor, top)


def split(value):
    high = value.astype(BF16)
    return high, (value - high.astype(F32)).astype(BF16)


def product_kernel(low_ref, trailing_ref, vectors_ref, out_ref, both):
    del low_ref
    part = pl.program_id(1)
    width = out_ref.shape[1]

    @pl.when(pl.program_id(0) == 0)
    def _():
        high, low = split(vectors_ref[0])
        both[part, :, :width] = high
        both[part, :, width:] = low

    high, low = split(trailing_ref[...])
    right = both[part]
    value = dot_fast(high, right) + dot_fast(low, right)
    value = value[:, :width] + value[:, width:]

    @pl.when(part == 0)
    def _():
        out_ref[...] = value

    @pl.when(part > 0)
    def _():
        out_ref[...] += value


def product(low, trailing, vectors):
    rows = trailing.shape[0]
    ratio, depth, width = vectors.shape
    tile = min(rows, 512)
    return pl.pallas_call(
        product_kernel,
        out_shape=jax.ShapeDtypeStruct((rows, width), F32),
        grid_spec=pltpu.PrefetchScalarGridSpec(
            num_scalar_prefetch=1,
            grid=(rows // tile, ratio),
            in_specs=[
                pl.BlockSpec((tile, depth), lambda i, t, low: (i, t ^ low[0])),
                pl.BlockSpec((1, depth, width), lambda i, t, low: (t, 0, 0)),
            ],
            out_specs=pl.BlockSpec((tile, width), lambda i, t, low: (i, 0)),
            scratch_shapes=[pltpu.VMEM((ratio, depth, 2 * width), BF16)],
        ),
        compiler_params=pltpu.CompilerParams(vmem_limit_bytes=48 * 1024 * 1024),
        name="product",
    )(low, trailing, vectors)


def update_kernel(low_ref, trailing_ref, left_ref, applied_ref, vectors_ref, out_ref, high_ref, rest_ref):
    del low_ref
    width = vectors_ref.shape[2]

    @pl.when(pl.program_id(1) == 0)
    def _():
        for place, ref in ((0, applied_ref), (width, vectors_ref)):
            high, rest = split(ref[0].T)
            high_ref[place : place + width, :] = high
            rest_ref[place : place + width, :] = rest

    high, rest = split(left_ref[...])
    value = dot_fast(high, high_ref[...]) + dot_fast(high, rest_ref[...]) + dot_fast(rest, high_ref[...])
    out_ref[...] = trailing_ref[...] - value


def update(low, trailing, left, applied, vectors):
    rows = trailing.shape[0]
    ratio, depth, width = vectors.shape
    tile = min(rows, 512)
    return pl.pallas_call(
        update_kernel,
        out_shape=jax.ShapeDtypeStruct(trailing.shape, F32),
        grid_spec=pltpu.PrefetchScalarGridSpec(
            num_scalar_prefetch=1,
            grid=(ratio, rows // tile),
            in_specs=[
                pl.BlockSpec((tile, depth), lambda t, i, low: (i, t ^ low[0])),
                pl.BlockSpec((tile, 2 * width), lambda t, i, low: (i, 0)),
                pl.BlockSpec((1, depth, width), lambda t, i, low: (t, 0, 0)),
                pl.BlockSpec((1, depth, width), lambda t, i, low: (t, 0, 0)),
            ],
            out_specs=pl.BlockSpec((tile, depth), lambda t, i, low: (i, t ^ low[0])),
            scratch_shapes=[pltpu.VMEM((2 * width, depth), BF16)] * 2,
        ),
        compiler_params=pltpu.CompilerParams(vmem_limit_bytes=48 * 1024 * 1024),
        name="update",
    )(low, trailing, left, applied, vectors)


def swap(value, axis, bit):
    count = lax.axis_size(axis)
    return lax.ppermute(value, axis, [(i, i ^ bit) for i in range(count)])


def bits_of(count):
    return [1 << b for b in range(count.bit_length() - 1)]


def sum_small(value, axis):
    for bit in bits_of(lax.axis_size(axis)):
        value = value + swap(value, axis, bit)
    return value


def sum_over_col(value):
    half = value.shape[0] // 2
    first, *others = bits_of(lax.axis_size("col"))
    mine = lax.axis_index("col") & 1
    keep = lax.dynamic_slice_in_dim(value, mine * half, half, 0)
    give = lax.dynamic_slice_in_dim(value, (1 - mine) * half, half, 0)
    keep = keep + swap(give, "col", first)
    for bit in others:
        keep = keep + swap(keep, "col", bit)
    other = swap(keep, "col", first)
    return jnp.where(mine == 0, jnp.concatenate([keep, other]), jnp.concatenate([other, keep]))


def gather_column_block(value):
    row_n, col_n = lax.axis_size("row"), lax.axis_size("col")
    ratio = row_n // col_n
    row, col = lax.axis_index("row"), lax.axis_index("col")
    done = 0
    away = (row // ratio) ^ col
    for bit in reversed(bits_of(col_n)):
        pairs = []
        for r in range(row_n):
            for c in range(col_n):
                if ((r // ratio) ^ c) & ~done == 0:
                    pairs.append((r * col_n + c, (r ^ (bit * ratio)) * col_n + c))
        moved = lax.ppermute(value, ("row", "col"), pairs)
        value = jnp.where((away & ~done) == bit, moved, value)
        done |= bit
    blocks = value[None]
    for bit in bits_of(ratio):
        blocks = jnp.concatenate([blocks, swap(blocks, "row", bit)])
    return blocks


def broadcast_col(value):
    col_n = lax.axis_size("col")
    col = lax.axis_index("col")
    for bit in bits_of(col_n):
        moved = lax.ppermute(value, "col", [(i, i + bit) for i in range(bit)])
        value = jnp.where((col >= bit) & (col < 2 * bit), moved, value)
    return value


def body(panel_block, trailing):
    shard_rows, width = panel_block.shape
    row, col = lax.axis_index("row"), lax.axis_index("col")
    ratio = lax.axis_size("row") // lax.axis_size("col")
    low = row % ratio
    low_arg = low.astype(jnp.int32)[None]

    first_gram = sum_small(dot_tn(panel_block, panel_block), "row")
    panel_blocks = gather_column_block(panel_block)
    top_panel = broadcast_col(
        lax.dynamic_index_in_dim(panel_blocks, low, 0, keepdims=False)[:width]
    )
    first_factor, first_inverse, first_basis, second_part = first_pass(first_gram, panel_block)
    second_gram = sum_small(second_part, "row")
    first_blocks = dot_nt(panel_blocks.reshape(-1, width), first_inverse)
    first_top = dot_nt(top_panel, first_inverse)
    raw = product(low_arg, trailing, first_blocks.reshape(ratio, shard_rows, width))

    second_inverse, band_block, kernel = second_pass(second_gram, first_factor, first_top)

    lane = jnp.arange(width)
    own_rows = row * shard_rows + jnp.arange(shard_rows)
    vectors = dot_nt(first_basis, second_inverse) + (own_rows[:, None] == lane).astype(F32)
    sub = jnp.arange(ratio) ^ low
    block_rows = (col * ratio + sub)[:, None] * shard_rows + jnp.arange(shard_rows)
    block_vectors = dot_nt(first_blocks, second_inverse).reshape(ratio, shard_rows, width)
    block_vectors = block_vectors + (block_rows[:, :, None] == lane).astype(F32)

    part = dot_nt(raw, second_inverse) + jnp.where(col == 0, trailing[:, :width], 0.0)
    own = sum_over_col(part)
    blocks = gather_column_block(own)
    inner = sum_small(dot_tn(vectors, own), "row")
    inner = dot_tn(kernel, dot_nn(inner, kernel))
    left = jnp.concatenate(
        [dot_nt(vectors, kernel), dot_nn(own, kernel) - dot_nn(vectors, inner)], axis=1
    )
    reduced = update(low_arg, trailing, left, blocks, block_vectors)
    return (reduced, band_block, first_factor)


def solution(mesh):
    in_specs = (P("row", None), P("row", "col"))
    out_specs = (P("row", "col"), P(), P())
    return jax.shard_map(body, mesh=mesh, in_specs=in_specs, out_specs=out_specs, check_vma=False)
```

time: 733 us -> 263 us (0.36)
  waiting for transfers between devices: 327 us -> 128 us
  other arithmetic: 167 us -> 13 us
  matrix products: 124 us -> 17.7 us
  local copies, waits for them, and re-layouts: 86.5 us -> 1.89 us
  Pallas kernels: 0 us -> 66.5 us
  starting transfers between devices: 1.06 us -> 30.4 us
  between operations: 14.6 us -> 0.97 us
    psum x5 -> x0, waiting for transfers between devices: 327 us -> none  [the longest x1 157 us: body(): col_product, col_vectors = lax.psum((partial_product, placed), 'row')]
    ppermute x0 -> x20, waiting for transfers between devices: none -> 128 us  [the longest x14 66 us: swap(): return lax.ppermute(value, axis, [(i, i ^ bit) for i in range(count)])]
    div x130 -> x0, other arithmetic: 107 us -> none  [the longest x128 105 us: eliminate(): pivot_row = pivot_row / pivot_row[pivot]]
    dot_general x52 -> x12, matrix products: 122 us -> 17.7 us  [the longest x6 9.13 us: dot_nt(): lax.dot_general(a, b, (((1,), (1,)), ((), ())), precision=HIGH, preferred...]
    dynamic_slice x128 -> x1, local copies, waits for them, and re-layouts: 74.9 us -> 1.88 us  [sum_over_col(): give = lax.dynamic_slice_in_dim(value, (1 - mine) * half, half, 0)]
    pallas_call x0 -> x4, Pallas kernels: none -> 66.5 us  [the longest x1 30.5 us: update(): pl.pallas_call(update_kernel, out_shape=jax.ShapeDtypeStruct(trailing.sha...]
    another operation x10 -> x0, other arithmetic: 45.6 us -> none  [the longest x4 20.9 us: right_solve(): lax.linalg.triangular_solve(factor, values, left_side=False, lower=True,...]
    ppermute x0 -> x20, starting transfers between devices: none -> 30.4 us  [the longest x14 23.4 us: swap(): return lax.ppermute(value, axis, [(i, i ^ bit) for i in range(count)])]
  transfers between devices with their start and end apart: 5 -> 20, of which waited for: 5 -> 14; matrix products, arithmetic and copies ran while one was open for 5% -> 8% of each run, Pallas kernels for 0% -> 9%
where the time goes in v1:
time: 263 us; the launch traced here: 258 us
  waiting for transfers between devices  128 us (49%)
  Pallas kernels  66.5 us (25%)
  starting transfers between devices  30.4 us (12%)
  matrix products  17.7 us (7%)
  other arithmetic  13 us (5%)
    ppermute x14, waiting for transfers between devices, swap(): return lax.ppermute(value, axis, [(i, i ^ bit) for i in range(count)])  66 us
    ppermute x4, waiting for transfers between devices, gather_column_block(): moved = lax.ppermute(value, ('row', 'col'), pairs)  61.8 us
    pallas_call x1, Pallas kernels, update(): pl.pallas_call(update_kernel, out_shape=jax.ShapeDtypeStruct(trailing.sha...  30.5 us
    ppermute x14, starting transfers between devices, swap(): return lax.ppermute(value, axis, [(i, i ^ bit) for i in range(count)])  23.4 us
    pallas_call x1, Pallas kernels, product(): pl.pallas_call(product_kernel, out_shape=jax.ShapeDtypeStruct((rows, widt...  16.3 us
    pallas_call x1, Pallas kernels, second_pass(): pl.pallas_call(second_kernel, out_shape=(square, square, square), compile...  11.8 us
    dot_general x6, matrix products, dot_nt(): lax.dot_general(a, b, (((1,), (1,)), ((), ())), precision=HIGH, preferred...  9.13 us
    pallas_call x1, Pallas kernels, first_pass(): pl.pallas_call(first_kernel, out_shape=(square, square, jax.ShapeDtypeStr...  7.94 us
  transfers between devices with their start and end apart: 20, of which 14 were waited for; matrix products, arithmetic and copies ran while one was open for 8% of the time, Pallas kernels for 9%

profile of v1, /device:TPU:12, one launch (start us, length us, event | category | flops | bytes accessed | tf_op | source)
XLA Modules:
  0.0 258.3 jit_solution(8655570043471998967)
XLA Ops:
  4.2 40.3 %collective-permute-done.7 = f32[2048,128]{1,0:T(8,128)} collective-permute-done((f32[2048,128]{1,0:T(8,128)S(1)}, f32[2048,128]{1,0:T(8,128)}, u32[]{:S(2)}, u32[]{:S(2)}) %collective-permute-start.7) | collective-permute-done | bytes 1048608 | tf_op jit(solution)/shard_map/ppermute | solution.py:293
  49.8 15.7 %collective-permute-done = f32[128,128]{1,0:T(8,128)S(1)} collective-permute-done((f32[128,128]{1,0:T(8,128)S(1)}, f32[128,128]{1,0:T(8,128)S(1)}, u32[]{:S(2)}, u32[]{:S(2)}) %collective-permute-start) | collective-permute-done | bytes 65568 | tf_op jit(solution)/shard_map/ppermute | solution.py:255
  65.5 3.6 %collective-permute-start.1 = (f32[128,128]{1,0:T(8,128)S(1)}, f32[128,128]{1,0:T(8,128)S(1)}, u32[]{:S(2)}, u32[]{:S(2)}) collective-permute-start(f32[128,128]{1,0:T(8,128)S(1)} %add.95), channel_id=1, source_target_pairs={{0,8},{4,12},{8,0},{12,4},{16,24},{20,28},{24,16},{28,20},{1,9},{5... | collective-permute-start | bytes 196616 | tf_op jit(solution)/shard_map/ppermute | solution.py:255
  69.1 2.8 %collective-permute-done.1 = f32[128,128]{1,0:T(8,128)S(1)} collective-permute-done((f32[128,128]{1,0:T(8,128)S(1)}, f32[128,128]{1,0:T(8,128)S(1)}, u32[]{:S(2)}, u32[]{:S(2)}) %collective-permute-start.1) | collective-permute-done | bytes 65568 | tf_op jit(solution)/shard_map/ppermute | solution.py:255
  72.0 5.3 %collective-permute-done.2 = f32[128,128]{1,0:T(8,128)S(1)} collective-permute-done((f32[128,128]{1,0:T(8,128)S(1)}, f32[128,128]{1,0:T(8,128)S(1)}, u32[]{:S(2)}, u32[]{:S(2)}) %collective-permute-start.2) | collective-permute-done | bytes 65568 | tf_op jit(solution)/shard_map/ppermute | solution.py:255
  77.3 7.9 %first_pass.1 = (f32[128,128]{1,0:T(8,128)}, f32[128,128]{1,0:T(8,128)S(1)}, f32[2048,128]{1,0:T(8,128)S(1)}, f32[128,128]{1,0:T(8,128)S(1)}) custom-call(f32[128,128]{1,0:T(8,128)S(1)} %add.97.gram_ref, f32[2048,128]{1,0:T(8,128)S(1)} %copy-done), custom_call_target="tpu_custom_call" | custom-call | tf_op jit(solution)/shard_map/first_pass/pallas_call | solution.py:131
  86.7 2.8 %collective-permute-done.3 = f32[128,128]{1,0:T(8,128)S(1)} collective-permute-done((f32[128,128]{1,0:T(8,128)S(1)}, f32[128,128]{1,0:T(8,128)S(1)}, u32[]{:S(2)}, u32[]{:S(2)}) %collective-permute-start.3) | collective-permute-done | bytes 65568 | tf_op jit(solution)/shard_map/ppermute | solution.py:255
  94.0 5.1 %collective-permute-done.5 = f32[128,128]{1,0:T(8,128)S(1)} collective-permute-done((f32[128,128]{1,0:T(8,128)S(1)}, f32[128,128]{1,0:T(8,128)S(1)}, u32[]{:S(2)}, u32[]{:S(2)}) %collective-permute-start.5) | collective-permute-done | bytes 65568 | tf_op jit(solution)/shard_map/ppermute | solution.py:255
  104.4 16.3 %product.1 = f32[2048,128]{1,0:T(8,128)S(1)} custom-call(s32[1]{0:T(128)} %bitcast.low_ref, f32[2048,4096]{1,0:T(8,128)} %trailing_ref.3, f32[2,2048,128]{2,1,0:T(8,128)S(1)} %bitcast.32), custom_call_target="tpu_custom_call" | custom-call | tf_op jit(solution)/shard_map/product/pallas_call | solution.py:195
  120.9 11.8 %second_pass.1 = (f32[128,128]{1,0:T(8,128)S(1)}, f32[128,128]{1,0:T(8,128)}, f32[128,128]{1,0:T(8,128)S(1)}) custom-call(f32[128,128]{1,0:T(8,128)S(1)} %add.100.gram_ref, f32[128,128]{1,0:T(8,128)S(1)} %copy-done.1, f32[128,128]{1,0:T(8,128)S(1)} %fusion.3.top_ref), custom_call_target="tpu_custom_call" | custom-call | tf_op jit(solution)/shard_map/second_pass/pallas_call | solution.py:153
  132.7 3.2 %convolution_add_fusion = f32[2048,128]{1,0:T(8,128)} fusion(f32[2048,128]{1,0:T(8,128)S(1)} %product.1, f32[128,128]{1,0:T(8,128)S(1)} %get-tuple-element.14, f32[2048,4096]{1,0:T(8,128)} %trailing_ref.3, pred[]{:T(512)S(6)} %eq.48), kind=kOutput, calls=%fused_computation.4 | convolution fusion | flops 403177472 | bytes 3211265 | tf_op jit(solution)/shard_map/dot_general | solution.py:21
  137.8 2.2 collective-permute-done.11
  141.3 2.7 %collective-permute-start.12 = (f32[1024,128]{1,0:T(8,128)S(1)}, f32[1024,128]{1,0:T(8,128)S(1)}, u32[]{:S(2)}, u32[]{:S(2)}) collective-permute-start(f32[1024,128]{1,0:T(8,128)S(1)} %dynamic-slice_add_fusion), channel_id=1, source_target_pairs={{0,2},{1,3},{2,0},{3,1},{4,6},{5,7},{6,4},{7,5},{8,10},{9,11},{10,... | collective-permute-start | bytes 1572872 | tf_op jit(solution)/shard_map/ppermute | solution.py:255
  144.0 12.2 %collective-permute-done.12 = f32[1024,128]{1,0:T(8,128)S(1)} collective-permute-done((f32[1024,128]{1,0:T(8,128)S(1)}, f32[1024,128]{1,0:T(8,128)S(1)}, u32[]{:S(2)}, u32[]{:S(2)}) %collective-permute-start.12) | collective-permute-done | bytes 524320 | tf_op jit(solution)/shard_map/ppermute | solution.py:255
  159.3 2.6 %maximum_select_fusion = f32[2048,128]{1,0:T(8,128)} fusion(f32[1024,128]{1,0:T(8,128)} %collective-permute-done.13, f32[1024,128]{1,0:T(8,128)} %add.109, pred[]{:T(512)S(6)} %eq.47), kind=kLoop, calls=%fused_computation.10 | loop fusion | flops 786432 | bytes 2097153 | tf_op jit(solution)/shard_map/jit(_where)/select_n | solution.py:278
  164.7 3.1 %fusion.10 = f32[128,128]{1,0:T(8,128)S(1)} fusion(f32[2048,128]{1,0:T(8,128)S(1)} %convolution_add_fusion.1, f32[2048,128]{1,0:T(8,128)} %maximum_select_fusion), kind=kOutput, calls=%fused_computation.32 | convolution fusion | flops 402653184 | bytes 2162688 | tf_op jit(solution)/shard_map/dot_general | solution.py:25
  167.8 2.4 collective-permute-start.14
  172.4 2.4 collective-permute-start.15
  177.4 2.3 convert_add_fusion.vectors_ref
  179.8 4.1 %collective-permute-start.16 = (f32[128,128]{1,0:T(8,128)S(1)}, f32[128,128]{1,0:T(8,128)S(1)}, u32[]{:S(2)}, u32[]{:S(2)}) collective-permute-start(f32[128,128]{1,0:T(8,128)S(1)} %add.111), channel_id=1, source_target_pairs={{0,16},{4,20},{8,24},{12,28},{16,0},{20,4},{24,8},{28,12},{1,17},{... | collective-permute-start | bytes 196616 | tf_op jit(solution)/shard_map/ppermute | solution.py:255
  187.1 21.5 %collective-permute-done.18 = f32[2048,128]{1,0:T(8,128)S(1)} collective-permute-done((f32[2048,128]{1,0:T(8,128)S(1)}, f32[2048,128]{1,0:T(8,128)S(1)}, u32[]{:S(2)}, u32[]{:S(2)}) %collective-permute-start.18) | collective-permute-done | bytes 1048608 | tf_op jit(solution)/shard_map/ppermute | solution.py:293
  208.7 2.4 collective-permute-start.19
  214.7 13.0 %collective-permute-done.19 = f32[1,2048,128]{2,1,0:T(8,128)S(1)} collective-permute-done((f32[1,2048,128]{2,1,0:T(8,128)S(1)}, f32[1,2048,128]{2,1,0:T(8,128)S(1)}, u32[]{:S(2)}, u32[]{:S(2)}) %collective-permute-start.19) | collective-permute-done | bytes 1048608 | tf_op jit(solution)/shard_map/ppermute | solution.py:255
  227.8 30.5 %update.1 = f32[2048,4096]{1,0:T(8,128)} custom-call(s32[1]{0:T(128)} %bitcast.low_ref, f32[2048,4096]{1,0:T(8,128)} %trailing_ref.3, f32[2048,256]{1,0:T(8,128)S(1)} %pad_maximum_fusion.1.left_ref, f32[2,2048,128]{2,1,0:T(8,128)S(1)} %pad_maximum_fusion.2.applied_ref, f32[2,2048,128]{2,1,0:T(8,128)} %convert_add_fusion.vectors_ref), custom_call_target="tpu_custom_call" | custom-call | tf_op jit(solution)/shard_map/update/pallas_call | solution.py:233
  (61 shorter events, 41.2 us)
Async XLA Ops:
  0.6 0.8 collective-permute-start.6
  2.7 44.7 %copy-start = (f32[2048,128]{1,0:T(8,128)S(1)}, f32[2048,128]{1,0:T(8,128)}, u32[]{:S(2)}) copy-start(f32[2048,128]{1,0:T(8,128)} %panel_ref.1) | copy-start | bytes 3145732
  2.8 41.8 %collective-permute-start.7 = (f32[2048,128]{1,0:T(8,128)S(1)}, f32[2048,128]{1,0:T(8,128)}, u32[]{:S(2)}, u32[]{:S(2)}) collective-permute-start(f32[2048,128]{1,0:T(8,128)S(1)} %broadcast_select_fusion.1), channel_id=1, source_target_pairs={{0,8},{2,10},{4,12},{6,14},{9,1},{11,3},{13,5},{15,7},{16,24},{18,... | collective-permute-start | bytes 3145736 | tf_op jit(solution)/shard_map/ppermute | solution.py:293
  45.9 53.3 %collective-permute-start.8 = (f32[1,2048,128]{2,1,0:T(8,128)S(1)}, f32[1,2048,128]{2,1,0:T(8,128)}, u32[]{:S(2)}, u32[]{:S(2)}) collective-permute-start(f32[1,2048,128]{2,1,0:T(8,128)S(1)} %select_bitcast_fusion.1), channel_id=1, source_target_pairs={{0,4},{4,0},{8,12},{12,8},{16,20},{20,16},{24,28},{28,24},{1,5},{5... | collective-permute-start | bytes 3145736 | tf_op jit(solution)/shard_map/ppermute | solution.py:255
  49.2 16.3 %collective-permute-start = (f32[128,128]{1,0:T(8,128)S(1)}, f32[128,128]{1,0:T(8,128)S(1)}, u32[]{:S(2)}, u32[]{:S(2)}) collective-permute-start(f32[128,128]{1,0:T(8,128)S(1)} %fusion.7), channel_id=1, source_target_pairs={{0,4},{4,0},{8,12},{12,8},{16,20},{20,16},{24,28},{28,24},{1,5},{5... | collective-permute-start | bytes 196616 | tf_op jit(solution)/shard_map/ppermute | solution.py:255
  65.5 6.4 %collective-permute-start.1 = (f32[128,128]{1,0:T(8,128)S(1)}, f32[128,128]{1,0:T(8,128)S(1)}, u32[]{:S(2)}, u32[]{:S(2)}) collective-permute-start(f32[128,128]{1,0:T(8,128)S(1)} %add.95), channel_id=1, source_target_pairs={{0,8},{4,12},{8,0},{12,4},{16,24},{20,28},{24,16},{28,20},{1,9},{5... | collective-permute-start | bytes 196616 | tf_op jit(solution)/shard_map/ppermute | solution.py:255
  72.0 5.3 %collective-permute-start.2 = (f32[128,128]{1,0:T(8,128)S(1)}, f32[128,128]{1,0:T(8,128)S(1)}, u32[]{:S(2)}, u32[]{:S(2)}) collective-permute-start(f32[128,128]{1,0:T(8,128)S(1)} %add.96), channel_id=1, source_target_pairs={{0,16},{4,20},{8,24},{12,28},{16,0},{20,4},{24,8},{28,12},{1,17},{... | collective-permute-start | bytes 196616 | tf_op jit(solution)/shard_map/ppermute | solution.py:255
  85.3 4.3 %collective-permute-start.3 = (f32[128,128]{1,0:T(8,128)S(1)}, f32[128,128]{1,0:T(8,128)S(1)}, u32[]{:S(2)}, u32[]{:S(2)}) collective-permute-start(f32[128,128]{1,0:T(8,128)S(1)} %get-tuple-element.11), channel_id=1, source_target_pairs={{0,4},{4,0},{8,12},{12,8},{16,20},{20,16},{24,28},{28,24},{1,5},{5... | collective-permute-start | bytes 196616 | tf_op jit(solution)/shard_map/ppermute | solution.py:255
  89.5 4.3 %collective-permute-start.4 = (f32[128,128]{1,0:T(8,128)S(1)}, f32[128,128]{1,0:T(8,128)S(1)}, u32[]{:S(2)}, u32[]{:S(2)}) collective-permute-start(f32[128,128]{1,0:T(8,128)S(1)} %add.98), channel_id=1, source_target_pairs={{0,8},{4,12},{8,0},{12,4},{16,24},{20,28},{24,16},{28,20},{1,9},{5... | collective-permute-start | bytes 196616 | tf_op jit(solution)/shard_map/ppermute | solution.py:255
  93.9 5.2 %collective-permute-start.5 = (f32[128,128]{1,0:T(8,128)S(1)}, f32[128,128]{1,0:T(8,128)S(1)}, u32[]{:S(2)}, u32[]{:S(2)}) collective-permute-start(f32[128,128]{1,0:T(8,128)S(1)} %add.99), channel_id=1, source_target_pairs={{0,16},{4,20},{8,24},{12,28},{16,0},{20,4},{24,8},{28,12},{1,17},{... | collective-permute-start | bytes 196616 | tf_op jit(solution)/shard_map/ppermute | solution.py:255
  99.2 2.0 collective-permute-start.9
  101.2 19.4 %collective-permute-start.10 = (f32[128,128]{1,0:T(8,128)S(1)}, f32[128,128]{1,0:T(8,128)S(1)}, u32[]{:S(2)}, u32[]{:S(2)}) collective-permute-start(f32[128,128]{1,0:T(8,128)S(1)} %broadcast_select_fusion.2), channel_id=1, source_target_pairs={{0,2},{1,3},{4,6},{5,7},{8,10},{9,11},{12,14},{13,15},{16,18},{17,... | collective-permute-start | bytes 196616 | tf_op jit(solution)/shard_map/ppermute | solution.py:306
  104.4 16.6 %copy-start.1 = (f32[128,128]{1,0:T(8,128)S(1)}, f32[128,128]{1,0:T(8,128)}, u32[]{:S(2)}) copy-start(f32[128,128]{1,0:T(8,128)} %get-tuple-element.9.first_ref) | copy-start | bytes 196612
  137.8 2.3 collective-permute-start.11
  141.3 14.9 %collective-permute-start.12 = (f32[1024,128]{1,0:T(8,128)S(1)}, f32[1024,128]{1,0:T(8,128)S(1)}, u32[]{:S(2)}, u32[]{:S(2)}) collective-permute-start(f32[1024,128]{1,0:T(8,128)S(1)} %dynamic-slice_add_fusion), channel_id=1, source_target_pairs={{0,2},{1,3},{2,0},{3,1},{4,6},{5,7},{6,4},{7,5},{8,10},{9,11},{10,... | collective-permute-start | bytes 1572872 | tf_op jit(solution)/shard_map/ppermute | solution.py:255
  157.0 2.3 collective-permute-start.13
  161.9 12.9 %collective-permute-start.17 = (f32[2048,128]{1,0:T(8,128)}, f32[2048,128]{1,0:T(8,128)}, u32[]{:S(2)}, u32[]{:S(2)}) collective-permute-start(f32[2048,128]{1,0:T(8,128)} %maximum_select_fusion), channel_id=1, source_target_pairs={{0,16},{4,20},{9,25},{13,29},{18,2},{22,6},{27,11},{31,15}} | collective-permute-start | bytes 3145736 | tf_op jit(solution)/shard_map/ppermute | solution.py:293
  167.8 4.6 %collective-permute-start.14 = (f32[128,128]{1,0:T(8,128)S(1)}, f32[128,128]{1,0:T(8,128)S(1)}, u32[]{:S(2)}, u32[]{:S(2)}) collective-permute-start(f32[128,128]{1,0:T(8,128)S(1)} %fusion.10), channel_id=1, source_target_pairs={{0,4},{4,0},{8,12},{12,8},{16,20},{20,16},{24,28},{28,24},{1,5},{5... | collective-permute-start | bytes 196616 | tf_op jit(solution)/shard_map/ppermute | solution.py:255
  172.4 7.3 %collective-permute-start.15 = (f32[128,128]{1,0:T(8,128)S(1)}, f32[128,128]{1,0:T(8,128)S(1)}, u32[]{:S(2)}, u32[]{:S(2)}) collective-permute-start(f32[128,128]{1,0:T(8,128)S(1)} %add.110), channel_id=1, source_target_pairs={{0,8},{4,12},{8,0},{12,4},{16,24},{20,28},{24,16},{28,20},{1,9},{5... | collective-permute-start | bytes 196616 | tf_op jit(solution)/shard_map/ppermute | solution.py:255
  176.1 32.4 %collective-permute-start.18 = (f32[2048,128]{1,0:T(8,128)S(1)}, f32[2048,128]{1,0:T(8,128)S(1)}, u32[]{:S(2)}, u32[]{:S(2)}) collective-permute-start(f32[2048,128]{1,0:T(8,128)S(1)} %broadcast_select_fusion), channel_id=1, source_target_pairs={{0,8},{2,10},{4,12},{6,14},{9,1},{11,3},{13,5},{15,7},{16,24},{18,... | collective-permute-start | bytes 3145736 | tf_op jit(solution)/shard_map/ppermute | solution.py:293
  179.8 7.1 %collective-permute-start.16 = (f32[128,128]{1,0:T(8,128)S(1)}, f32[128,128]{1,0:T(8,128)S(1)}, u32[]{:S(2)}, u32[]{:S(2)}) collective-permute-start(f32[128,128]{1,0:T(8,128)S(1)} %add.111), channel_id=1, source_target_pairs={{0,16},{4,20},{8,24},{12,28},{16,0},{20,4},{24,8},{28,12},{1,17},{... | collective-permute-start | bytes 196616 | tf_op jit(solution)/shard_map/ppermute | solution.py:255
  208.7 19.0 %collective-permute-start.19 = (f32[1,2048,128]{2,1,0:T(8,128)S(1)}, f32[1,2048,128]{2,1,0:T(8,128)S(1)}, u32[]{:S(2)}, u32[]{:S(2)}) collective-permute-start(f32[1,2048,128]{2,1,0:T(8,128)S(1)} %select_bitcast_fusion), channel_id=1, source_target_pairs={{0,4},{4,0},{8,12},{12,8},{16,20},{20,16},{24,28},{28,24},{1,5},{5... | collective-permute-start | bytes 3145736 | tf_op jit(solution)/shard_map/ppermute | solution.py:255
